TPU v7x, 32 devices: a whole 2x2x4 slice. The times are simulated.
32 devices in a mesh: gx: 8 (over z, y), gy: 4 (over x, core).
Axes of the slice: x: 2, y: 2, z: 4, core: 2. Of those that a mesh axis runs over, the one named last changes fastest.
Arguments:
- state: float32 [5, 120, 16384], P(None, None, ('gx', 'gy')), may hold values from -6 to 6
- coef: float32 [5, 5, 16384], P(None, None, ('gx', 'gy')), may hold values from -3 to 3
- basis_quad: float32 [216, 120], replicated, may hold values from -0.5 to 0.5
- test_deriv: float32 [120, 216], replicated, may hold values from -0.3125 to 0.3125
- trace_vec: float32 [120], replicated, may hold values from -0.5 to 0.5
- lift_vec: float32 [120], replicated, may hold values from -3 to 3
- tent_height: float32 [3, 2048], P(None, ('gx', 'gy')), may hold values from 0.2 to 0.4
- elem_tent: int32 [3, 16384], P(None, ('gx', 'gy')), may hold values from 0 to 2047, as said below
Outputs:
- final_state: float32 [5, 120, 16384], P(None, None, ('gx', 'gy'))
Inputs may be any that keep to these rules, and one draw needn't show every extreme that they name: `elem_tent`: tent t is owned by device t // 64 of the devices numbered with gx slowest. At every level the owner of an element's tent is the element's own device or one of its four neighbours along gx or gy, with wrap-around. At a level no device hands more than 64 of its elements to one neighbour; in every level some device hands exactly 64 to a neighbour, and some device receives exactly 64 from each of its four neighbours.
All inputs are finite; a program needn't handle non-finite values.
Results may differ from a plain program's by a relative error of at most 0.00011.
Values sent between devices are 32-bit elements; how exact they have to be, the bound alone decides.
A program may use at most 128 MiB of HBM per device.

v0:
```python
import jax
import jax.numpy as jnp
from jax import lax
from jax.sharding import PartitionSpec as P

HIGHEST = lax.Precision.HIGHEST


def from_behind(x, axis, by):
    peers = lax.axis_size(axis)
    return lax.ppermute(x, axis, [(i, (i + by) % peers) for i in range(peers)])


def select_dot(left, right):
    return jnp.dot(left, right, precision=HIGHEST, preferred_element_type=jnp.float32)


def pack_tents(tent_local, selector):
    marked = jnp.where(selector > 0.0, (tent_local + 1)[:, None], 0)
    return jnp.sum(marked, axis=0) - 1


def trace_values(values, trace_vec):
    return jnp.einsum(
        "b,fbs->fs", trace_vec, values, precision=HIGHEST, preferred_element_type=jnp.float32
    )


def derivative(values, coef_all, means, traces, basis_quad, test_deriv, lift_vec):
    at_points = jnp.einsum(
        "qb,fbs->fqs", basis_quad, values, precision=HIGHEST, preferred_element_type=jnp.float32
    )
    fields = values.shape[0]
    fluxes = []
    for target in range(fields):
        running = coef_all[target, 0][None, :] * at_points[0]
        for source in range(1, fields):
            running = running + coef_all[target, source][None, :] * at_points[source]
        fluxes.append(running)
    flux_all = jnp.stack(fluxes)
    weak_form = jnp.einsum(
        "bq,gqs->gbs", test_deriv, flux_all, precision=HIGHEST, preferred_element_type=jnp.float32
    )
    return weak_form + lift_vec[None, :, None] * (means - traces)[:, None, :]


def move_tents_first(payload, offset):
    return from_behind(payload, "gx", offset)


def move_tents_second(payload, offset):
    return from_behind(payload, "gy", offset)


def move_states_first(payload, offset):
    return from_behind(payload, "gx", offset)


def move_states_second(payload, offset):
    return from_behind(payload, "gy", offset)


def move_back_first(payload, offset):
    return from_behind(payload, "gx", offset)


def move_back_second(payload, offset):
    return from_behind(payload, "gy", offset)


def spread(payloads, first_mover, second_mover, offset):
    return [
        first_mover(payloads[0], offset),
        first_mover(payloads[1], -offset),
        second_mover(payloads[2], offset),
        second_mover(payloads[3], -offset),
    ]


def per_device(state, coef, basis_quad, test_deriv, trace_vec, lift_vec, tent_height, elem_tent):
    size_first = lax.axis_size("gx")
    size_second = lax.axis_size("gy")
    index_first = lax.axis_index("gx")
    index_second = lax.axis_index("gy")
    fields, basis, n_elem = state.shape
    tent_dev = tent_height.shape[1]
    capacity = n_elem // 8
    flat_coef = coef.reshape(fields * fields, n_elem)
    slot_iota = jnp.arange(capacity, dtype=jnp.int32)
    tent_iota = jnp.arange(tent_dev, dtype=jnp.int32)
    values = state
    for level_index in range(elem_tent.shape[0]):
        tents = elem_tent[level_index]
        owner = tents // tent_dev
        tent_local = tents - owner * tent_dev
        owner_first = owner // size_second
        owner_second = owner - owner_first * size_second
        same_first = owner_first == index_first
        same_second = owner_second == index_second
        stays = same_first & same_second
        keep = stays.astype(jnp.float32)
        heading = [
            (owner_first == (index_first + 1) % size_first) & same_second,
            (owner_first == (index_first + size_first - 1) % size_first) & same_second,
            same_first & (owner_second == (index_second + 1) % size_second),
            same_first & (owner_second == (index_second + size_second - 1) % size_second),
        ]
        selectors = []
        for route_mask in heading:
            position = jnp.cumsum(route_mask.astype(jnp.int32)) - 1
            selectors.append(
                (route_mask[:, None] & (position[:, None] == slot_iota[None, :])).astype(
                    jnp.float32
                )
            )
        sent_tents = spread(
            [pack_tents(tent_local, selector) for selector in selectors],
            move_tents_first,
            move_tents_second,
            1,
        )
        all_tents = jnp.concatenate([jnp.where(stays, tent_local, -1)] + sent_tents)
        member = (all_tents[:, None] == tent_iota[None, :]).astype(jnp.float32)
        safe_counts = jnp.maximum(jnp.sum(member, axis=0), 1.0)
        heights = select_dot(tent_height[level_index][None, :], member.T)[0]
        payload_flat = values.reshape(fields * basis, n_elem)
        outgoing = [
            (select_dot(payload_flat, selector), select_dot(flat_coef, selector))
            for selector in selectors
        ]
        incoming = spread(outgoing, move_states_first, move_states_second, 1)
        gathered = jnp.concatenate(
            [payload_flat * keep[None, :]] + [piece[0] for piece in incoming], axis=1
        ).reshape(fields, basis, -1)
        gathered_coef = jnp.concatenate(
            [flat_coef] + [piece[1] for piece in incoming], axis=1
        ).reshape(fields, fields, -1)
        current = gathered
        derivs = []
        for section_index in range(3):
            traces = trace_values(current, trace_vec)
            table = select_dot(traces, member) / safe_counts[None, :]
            means = select_dot(table, member.T)
            current = derivative(
                current, gathered_coef, means, traces, basis_quad, test_deriv, lift_vec
            )
            derivs.append(current)
        height_all = heights[None, None, :]
        updated = gathered + height_all * (
            derivs[0] + height_all / 2.0 * (derivs[1] + height_all / 3.0 * derivs[2])
        )
        flat_new = updated.reshape(fields * basis, -1)
        pieces = [
            flat_new[:, n_elem + route * capacity : n_elem + (route + 1) * capacity]
            for route in range(4)
        ]
        returned = spread(pieces, move_back_first, move_back_second, -1)
        merged = flat_new[:, :n_elem] * keep[None, :]
        for piece, selector in zip(returned, selectors):
            merged = merged + select_dot(piece, selector.T)
        values = merged.reshape(fields, basis, n_elem)
    return values


def solution(mesh):
    placed = (
        P(None, None, ("gx", "gy")),
        P(None, None, ("gx", "gy")),
        P(),
        P(),
        P(),
        P(),
        P(None, ("gx", "gy")),
        P(None, ("gx", "gy")),
    )
    return jax.shard_map(
        per_device,
        mesh=mesh,
        in_specs=placed,
        out_specs=P(None, None, ("gx", "gy")),
        check_vma=False,
    )
```

profile of v0, /device:TPU:0, one launch (start us, length us, event | category | flops | bytes accessed | tf_op | source)
XLA Modules:
  0.0 278.4 jit_solution(18017360248248699664)
XLA Ops:
  3.6 3.0 %collective-permute-start = (f32[600,64]{0,1:T(8,128)S(1)}, f32[600,64]{0,1:T(8,128)S(1)}, u32[]{:S(2)}, u32[]{:S(2)}) collective-permute-start(f32[600,64]{0,1:T(8,128)S(1)} %convolution_bitcast_fusion.12), channel_id=1, source_target_pairs={{0,4},{4,8},{8,12},{12,16},{16,20},{20,24},{24,28},{28,0},{1,5},{5... | collective-permute-start | bytes 460808 | tf_op jit(solution)/shard_map/ppermute | solution.py:11
  11.4 3.2 %collective-permute-start.5 = (s32[64]{0:T(128)}, s32[64]{0:T(128)}, u32[]{:S(2)}, u32[]{:S(2)}) collective-permute-start(s32[64]{0:T(128)} %broadcast_add_fusion.13), channel_id=1, source_target_pairs={{0,28},{4,0},{8,4},{12,8},{16,12},{20,16},{24,20},{28,24},{1,29},{... | collective-permute-start | bytes 776 | tf_op jit(solution)/shard_map/ppermute | solution.py:11
  36.8 4.7 %collective-permute-start.21 = (s32[64]{0:T(128)S(1)}, s32[64]{0:T(128)S(1)}, u32[]{:S(2)}, u32[]{:S(2)}) collective-permute-start(s32[64]{0:T(128)S(1)} %broadcast_add_fusion.9), channel_id=1, source_target_pairs={{0,28},{4,0},{8,4},{12,8},{16,12},{20,16},{24,20},{28,24},{1,29},{... | collective-permute-start | bytes 776 | tf_op jit(solution)/shard_map/ppermute | solution.py:11
  45.7 4.7 %collective-permute-start.37 = (s32[64]{0:T(128)S(1)}, s32[64]{0:T(128)S(1)}, u32[]{:S(2)}, u32[]{:S(2)}) collective-permute-start(s32[64]{0:T(128)S(1)} %broadcast_add_fusion.5), channel_id=1, source_target_pairs={{0,28},{4,0},{8,4},{12,8},{16,12},{20,16},{24,20},{28,24},{1,29},{... | collective-permute-start | bytes 776 | tf_op jit(solution)/shard_map/ppermute | solution.py:11
  54.2 4.7 %collective-permute-start.9 = (f32[25,64]{1,0:T(8,128)}, f32[25,64]{1,0:T(8,128)S(1)}, u32[]{:S(2)}, u32[]{:S(2)}) collective-permute-start(f32[25,64]{1,0:T(8,128)} %convolution_bitcast_fusion.23), channel_id=1, source_target_pairs={{0,28},{4,0},{8,4},{12,8},{16,12},{20,16},{24,20},{28,24},{1,29},{... | collective-permute-start | bytes 19208 | tf_op jit(solution)/shard_map/ppermute | solution.py:11
  68.3 2.8 %collective-permute-start.25 = (f32[25,64]{1,0:T(8,128)}, f32[25,64]{1,0:T(8,128)}, u32[]{:S(2)}, u32[]{:S(2)}) collective-permute-start(f32[25,64]{1,0:T(8,128)} %convolution_bitcast_fusion.19), channel_id=1, source_target_pairs={{0,28},{4,0},{8,4},{12,8},{16,12},{20,16},{24,20},{28,24},{1,29},{... | collective-permute-start | bytes 19208 | tf_op jit(solution)/shard_map/ppermute | solution.py:11
  79.0 2.9 %convolution_bitcast_fusion.8 = f32[5,216,768]{2,1,0:T(8,128)S(1)} fusion(f32[5,120,768]{2,1,0:T(8,128)S(1)} %bitcast.335, f32[216,120]{1,0:T(8,128)S(1)} %copy-done), kind=kOutput, calls=%fused_computation.8 | convolution fusion | flops 1194393600 | bytes 5264640 | tf_op jit(solution)/shard_map/qb,fbs->fqs/dot_general | solution.py:30
  88.9 2.8 %convolution_bitcast_fusion.7 = f32[5,216,768]{2,1,0:T(8,128)S(1)} fusion(f32[5,120,768]{2,1,0:T(8,128)S(1)} %bitcast_add_fusion.8, f32[216,120]{1,0:T(8,128)S(1)} %copy-done), kind=kOutput, calls=%fused_computation.7 | convolution fusion | flops 1194393600 | bytes 5264640 | tf_op jit(solution)/shard_map/qb,fbs->fqs/dot_general | solution.py:30
  93.4 12.4 %add_dynamic-update-slice_fusion.36 = f32[5,216,768]{2,1,0:T(8,128)S(1)} fusion(f32[5,216,768]{2,1,0:T(8,128)S(1)} %add_dynamic-update-slice_fusion.37, f32[5,216,768]{2,1,0:T(8,128)S(1)} %convolution_bitcast_fusion.7, f32[768]{0:T(1024)S(1)} %copy-done.16, f32[768]{0:T(1024)S(1)} %copy-done.17, f32[768]{0:T(1024)S(1)} %copy-done.18, ...), kind=kLoop, calls=%fused_computation.124 | loop fusion | flops 1492992 | bytes 4001792
  108.6 2.9 %convolution_bitcast_fusion.6 = f32[5,216,768]{2,1,0:T(8,128)S(1)} fusion(f32[5,120,768]{2,1,0:T(8,128)S(1)} %bitcast_add_fusion.7, f32[216,120]{1,0:T(8,128)S(1)} %copy-done), kind=kOutput, calls=%fused_computation.6 | convolution fusion | flops 1194393600 | bytes 5264640 | tf_op jit(solution)/shard_map/qb,fbs->fqs/dot_general | solution.py:30
  114.1 2.7 fusion.17
  123.0 4.7 %collective-permute-start.12 = (f32[600,64]{1,0:T(8,128)S(1)}, f32[600,64]{1,0:T(8,128)S(1)}, u32[]{:S(2)}, u32[]{:S(2)}) collective-permute-start(f32[600,64]{1,0:T(8,128)S(1)} %get-tuple-element.124), channel_id=1, source_target_pairs={{0,28},{4,0},{8,4},{12,8},{16,12},{20,16},{24,20},{28,24},{1,29},{... | collective-permute-start | bytes 460808 | tf_op jit(solution)/shard_map/ppermute | solution.py:11
  129.1 7.4 %collective-permute-done.13 = f32[600,64]{1,0:T(8,128)S(1)} collective-permute-done((f32[600,64]{1,0:T(8,128)S(1)}, f32[600,64]{1,0:T(8,128)S(1)}, u32[]{:S(2)}, u32[]{:S(2)}) %collective-permute-start.13) | collective-permute-done | bytes 153632 | tf_op jit(solution)/shard_map/ppermute | solution.py:11
  143.7 4.2 %collective-permute-start.17 = (f32[600,64]{1,0:T(8,128)S(1)}, f32[600,64]{1,0:T(8,128)S(1)}, u32[]{:S(2)}, u32[]{:S(2)}) collective-permute-start(f32[600,64]{1,0:T(8,128)S(1)} %fusion.55), channel_id=1, source_target_pairs={{0,28},{4,0},{8,4},{12,8},{16,12},{20,16},{24,20},{28,24},{1,29},{... | collective-permute-start | bytes 460808 | tf_op jit(solution)/shard_map/ppermute | solution.py:11
  149.9 6.6 %collective-permute-done.16 = f32[600,64]{1,0:T(8,128)S(1)} collective-permute-done((f32[600,64]{1,0:T(8,128)S(1)}, f32[600,64]{1,0:T(8,128)S(1)}, u32[]{:S(2)}, u32[]{:S(2)}) %collective-permute-start.16) | collective-permute-done | bytes 153632 | tf_op jit(solution)/shard_map/ppermute | solution.py:11
  156.5 6.2 %collective-permute-start.41 = (f32[25,64]{1,0:T(8,128)}, f32[25,64]{1,0:T(8,128)S(1)}, u32[]{:S(2)}, u32[]{:S(2)}) collective-permute-start(f32[25,64]{1,0:T(8,128)} %convolution_bitcast_fusion.15), channel_id=1, source_target_pairs={{0,28},{4,0},{8,4},{12,8},{16,12},{20,16},{24,20},{28,24},{1,29},{... | collective-permute-start | bytes 19208 | tf_op jit(solution)/shard_map/ppermute | solution.py:11
  165.2 2.8 %concatenate.61 = f32[600,768]{1,0:T(8,128)S(1)} concatenate(f32[600,512]{1,0:T(8,128)S(1)} %get-tuple-element.167, f32[600,64]{1,0:T(8,128)} %copy-done.8, f32[600,64]{1,0:T(8,128)} %copy-done.9, f32[600,64]{1,0:T(8,128)} %copy-done.10, f32[600,64]{1,0:T(8,128)} %copy-done.11), dimensions={1} | concatenate | bytes 3686400 | tf_op jit(solution)/shard_map/concatenate | solution.py:132
  168.0 2.9 %convolution_bitcast_fusion.5 = f32[5,216,768]{2,1,0:T(8,128)S(1)} fusion(f32[5,120,768]{2,1,0:T(8,128)S(1)} %bitcast.338, f32[216,120]{1,0:T(8,128)S(1)} %copy-done), kind=kOutput, calls=%fused_computation.5 | convolution fusion | flops 1194393600 | bytes 5264640 | tf_op jit(solution)/shard_map/qb,fbs->fqs/dot_general | solution.py:30
  175.6 2.8 %convolution_bitcast_fusion.4 = f32[5,216,768]{2,1,0:T(8,128)S(1)} fusion(f32[5,120,768]{2,1,0:T(8,128)S(1)} %bitcast_add_fusion.5, f32[216,120]{1,0:T(8,128)S(1)} %copy-done), kind=kOutput, calls=%fused_computation.4 | convolution fusion | flops 1194393600 | bytes 5264640 | tf_op jit(solution)/shard_map/qb,fbs->fqs/dot_general | solution.py:30
  183.3 2.9 %convolution_bitcast_fusion.3 = f32[5,216,768]{2,1,0:T(8,128)S(1)} fusion(f32[5,120,768]{2,1,0:T(8,128)S(1)} %bitcast_add_fusion.4, f32[216,120]{1,0:T(8,128)S(1)} %copy-done), kind=kOutput, calls=%fused_computation.3 | convolution fusion | flops 1194393600 | bytes 5264640 | tf_op jit(solution)/shard_map/qb,fbs->fqs/dot_general | solution.py:30
  188.8 2.7 fusion.11
  195.8 4.7 %collective-permute-start.28 = (f32[600,64]{1,0:T(8,128)S(1)}, f32[600,64]{1,0:T(8,128)S(1)}, u32[]{:S(2)}, u32[]{:S(2)}) collective-permute-start(f32[600,64]{1,0:T(8,128)S(1)} %get-tuple-element.120), channel_id=1, source_target_pairs={{0,28},{4,0},{8,4},{12,8},{16,12},{20,16},{24,20},{28,24},{1,29},{... | collective-permute-start | bytes 460808 | tf_op jit(solution)/shard_map/ppermute | solution.py:11
  203.1 4.6 %collective-permute-done.29 = f32[600,64]{1,0:T(8,128)S(1)} collective-permute-done((f32[600,64]{1,0:T(8,128)S(1)}, f32[600,64]{1,0:T(8,128)S(1)}, u32[]{:S(2)}, u32[]{:S(2)}) %collective-permute-start.29) | collective-permute-done | bytes 153632 | tf_op jit(solution)/shard_map/ppermute | solution.py:11
  214.9 4.2 %collective-permute-start.33 = (f32[600,64]{1,0:T(8,128)S(1)}, f32[600,64]{1,0:T(8,128)S(1)}, u32[]{:S(2)}, u32[]{:S(2)}) collective-permute-start(f32[600,64]{1,0:T(8,128)S(1)} %fusion.78), channel_id=1, source_target_pairs={{0,28},{4,0},{8,4},{12,8},{16,12},{20,16},{24,20},{28,24},{1,29},{... | collective-permute-start | bytes 460808 | tf_op jit(solution)/shard_map/ppermute | solution.py:11
  221.1 7.1 %collective-permute-done.32 = f32[600,64]{1,0:T(8,128)S(1)} collective-permute-done((f32[600,64]{1,0:T(8,128)S(1)}, f32[600,64]{1,0:T(8,128)S(1)}, u32[]{:S(2)}, u32[]{:S(2)}) %collective-permute-start.32) | collective-permute-done | bytes 153632 | tf_op jit(solution)/shard_map/ppermute | solution.py:11
  231.9 2.8 %concatenate.68 = f32[600,768]{1,0:T(8,128)S(1)} concatenate(f32[600,512]{1,0:T(8,128)S(1)} %get-tuple-element.169, f32[600,64]{1,0:T(8,128)} %copy-done.12, f32[600,64]{1,0:T(8,128)} %copy-done.13, f32[600,64]{1,0:T(8,128)} %copy-done.14, f32[600,64]{1,0:T(8,128)} %copy-done.15), dimensions={1} | concatenate | bytes 3686400 | tf_op jit(solution)/shard_map/concatenate | solution.py:132
  234.8 2.9 %convolution_bitcast_fusion.2 = f32[5,216,768]{2,1,0:T(8,128)S(1)} fusion(f32[5,120,768]{2,1,0:T(8,128)S(1)} %bitcast.341, f32[216,120]{1,0:T(8,128)S(1)} %copy-done), kind=kOutput, calls=%fused_computation.2 | convolution fusion | flops 1194393600 | bytes 5264640 | tf_op jit(solution)/shard_map/qb,fbs->fqs/dot_general | solution.py:30
  242.4 2.8 convolution_bitcast_fusion.1
  250.1 2.9 %convolution_bitcast_fusion = f32[5,216,768]{2,1,0:T(8,128)S(1)} fusion(f32[5,120,768]{2,1,0:T(8,128)S(1)} %bitcast_add_fusion.1, f32[216,120]{1,0:T(8,128)S(1)} %copy-done), kind=kOutput, calls=%fused_computation | convolution fusion | flops 1194393600 | bytes 5264640 | tf_op jit(solution)/shard_map/qb,fbs->fqs/dot_general | solution.py:30
  255.6 2.7 fusion.5
  260.7 4.3 %collective-permute-start.44 = (f32[600,64]{1,0:T(8,128)S(1)}, f32[600,64]{1,0:T(8,128)S(1)}, u32[]{:S(2)}, u32[]{:S(2)}) collective-permute-start(f32[600,64]{1,0:T(8,128)S(1)} %get-tuple-element.116), channel_id=1, source_target_pairs={{0,28},{4,0},{8,4},{12,8},{16,12},{20,16},{24,20},{28,24},{1,29},{... | collective-permute-start | bytes 460808 | tf_op jit(solution)/shard_map/ppermute | solution.py:11
  268.0 6.0 %collective-permute-done.45 = f32[600,64]{1,0:T(8,128)S(1)} collective-permute-done((f32[600,64]{1,0:T(8,128)S(1)}, f32[600,64]{1,0:T(8,128)S(1)}, u32[]{:S(2)}, u32[]{:S(2)}) %collective-permute-start.45) | collective-permute-done | bytes 153632 | tf_op jit(solution)/shard_map/ppermute | solution.py:11
  (562 shorter events, 141.2 us)
Async XLA Ops:
  3.6 64.6 %collective-permute-start = (f32[600,64]{0,1:T(8,128)S(1)}, f32[600,64]{0,1:T(8,128)S(1)}, u32[]{:S(2)}, u32[]{:S(2)}) collective-permute-start(f32[600,64]{0,1:T(8,128)S(1)} %convolution_bitcast_fusion.12), channel_id=1, source_target_pairs={{0,4},{4,8},{8,12},{12,16},{16,20},{20,24},{24,28},{28,0},{1,5},{5... | collective-permute-start | bytes 460808 | tf_op jit(solution)/shard_map/ppermute | solution.py:11
  9.3 27.4 %collective-permute-start.4 = (s32[64]{0:T(128)}, s32[64]{0:T(128)S(1)}, u32[]{:S(2)}, u32[]{:S(2)}) collective-permute-start(s32[64]{0:T(128)} %broadcast_add_fusion.14), channel_id=1, source_target_pairs={{0,4},{4,8},{8,12},{12,16},{16,20},{20,24},{24,28},{28,0},{1,5},{5... | collective-permute-start | bytes 776 | tf_op jit(solution)/shard_map/ppermute | solution.py:11
  11.4 25.4 %collective-permute-start.5 = (s32[64]{0:T(128)}, s32[64]{0:T(128)}, u32[]{:S(2)}, u32[]{:S(2)}) collective-permute-start(s32[64]{0:T(128)} %broadcast_add_fusion.13), channel_id=1, source_target_pairs={{0,28},{4,0},{8,4},{12,8},{16,12},{20,16},{24,20},{28,24},{1,29},{... | collective-permute-start | bytes 776 | tf_op jit(solution)/shard_map/ppermute | solution.py:11
  15.2 26.3 %collective-permute-start.6 = (s32[64]{0:T(128)}, s32[64]{0:T(128)}, u32[]{:S(2)}, u32[]{:S(2)}) collective-permute-start(s32[64]{0:T(128)} %broadcast_add_fusion.12), channel_id=1, source_target_pairs={{0,1},{1,2},{2,3},{3,0},{4,5},{5,6},{6,7},{7,4},{8,9},{9,10},{10,1... | collective-permute-start | bytes 776 | tf_op jit(solution)/shard_map/ppermute | solution.py:11
  15.7 25.8 %collective-permute-start.7 = (s32[64]{0:T(128)}, s32[64]{0:T(128)}, u32[]{:S(2)}, u32[]{:S(2)}) collective-permute-start(s32[64]{0:T(128)} %broadcast_add_fusion.11), channel_id=1, source_target_pairs={{0,3},{1,0},{2,1},{3,2},{4,7},{5,4},{6,5},{7,6},{8,11},{9,8},{10,9... | collective-permute-start | bytes 776 | tf_op jit(solution)/shard_map/ppermute | solution.py:11
  36.7 8.9 %collective-permute-start.20 = (s32[64]{0:T(128)S(1)}, s32[64]{0:T(128)S(1)}, u32[]{:S(2)}, u32[]{:S(2)}) collective-permute-start(s32[64]{0:T(128)S(1)} %broadcast_add_fusion.10), channel_id=1, source_target_pairs={{0,4},{4,8},{8,12},{12,16},{16,20},{20,24},{24,28},{28,0},{1,5},{5... | collective-permute-start | bytes 776 | tf_op jit(solution)/shard_map/ppermute | solution.py:11
  63.0 9.0 %collective-permute-start.1 = (f32[600,64]{0,1:T(8,128)S(1)}, f32[600,64]{0,1:T(8,128)S(1)}, u32[]{:S(2)}, u32[]{:S(2)}) collective-permute-start(f32[600,64]{0,1:T(8,128)S(1)} %convolution_bitcast_fusion.11), channel_id=1, source_target_pairs={{0,28},{4,0},{8,4},{12,8},{16,12},{20,16},{24,20},{28,24},{1,29},{... | collective-permute-start | bytes 460808 | tf_op jit(solution)/shard_map/ppermute | solution.py:11
  63.0 9.8 %collective-permute-start.2 = (f32[600,64]{0,1:T(8,128)S(1)}, f32[600,64]{0,1:T(8,128)S(1)}, u32[]{:S(2)}, u32[]{:S(2)}) collective-permute-start(f32[600,64]{0,1:T(8,128)S(1)} %convolution_bitcast_fusion.10), channel_id=1, source_target_pairs={{0,1},{1,2},{2,3},{3,0},{4,5},{5,6},{6,7},{7,4},{8,9},{9,10},{10,1... | collective-permute-start | bytes 460808 | tf_op jit(solution)/shard_map/ppermute | solution.py:11
  63.1 12.4 %collective-permute-start.3 = (f32[600,64]{0,1:T(8,128)S(1)}, f32[600,64]{0,1:T(8,128)S(1)}, u32[]{:S(2)}, u32[]{:S(2)}) collective-permute-start(f32[600,64]{0,1:T(8,128)S(1)} %convolution_bitcast_fusion.9), channel_id=1, source_target_pairs={{0,3},{1,0},{2,1},{3,2},{4,7},{5,4},{6,5},{7,6},{8,11},{9,8},{10,9... | collective-permute-start | bytes 460808 | tf_op jit(solution)/shard_map/ppermute | solution.py:11
  64.8 54.8 %collective-permute-start.24 = (f32[25,64]{1,0:T(8,128)}, f32[25,64]{1,0:T(8,128)}, u32[]{:S(2)}, u32[]{:S(2)}) collective-permute-start(f32[25,64]{1,0:T(8,128)} %convolution_bitcast_fusion.20), channel_id=1, source_target_pairs={{0,4},{4,8},{8,12},{12,16},{16,20},{20,24},{24,28},{28,0},{1,5},{5... | collective-permute-start | bytes 19208 | tf_op jit(solution)/shard_map/ppermute | solution.py:11
  68.3 52.1 %collective-permute-start.25 = (f32[25,64]{1,0:T(8,128)}, f32[25,64]{1,0:T(8,128)}, u32[]{:S(2)}, u32[]{:S(2)}) collective-permute-start(f32[25,64]{1,0:T(8,128)} %convolution_bitcast_fusion.19), channel_id=1, source_target_pairs={{0,28},{4,0},{8,4},{12,8},{16,12},{20,16},{24,20},{28,24},{1,29},{... | collective-permute-start | bytes 19208 | tf_op jit(solution)/shard_map/ppermute | solution.py:11
  72.0 49.1 %collective-permute-start.26 = (f32[25,64]{1,0:T(8,128)}, f32[25,64]{1,0:T(8,128)S(1)}, u32[]{:S(2)}, u32[]{:S(2)}) collective-permute-start(f32[25,64]{1,0:T(8,128)} %convolution_bitcast_fusion.18), channel_id=1, source_target_pairs={{0,1},{1,2},{2,3},{3,0},{4,5},{5,6},{6,7},{7,4},{8,9},{9,10},{10,1... | collective-permute-start | bytes 19208 | tf_op jit(solution)/shard_map/ppermute | solution.py:11
  72.8 48.3 %collective-permute-start.27 = (f32[25,64]{1,0:T(8,128)}, f32[25,64]{1,0:T(8,128)S(1)}, u32[]{:S(2)}, u32[]{:S(2)}) collective-permute-start(f32[25,64]{1,0:T(8,128)} %convolution_bitcast_fusion.17), channel_id=1, source_target_pairs={{0,3},{1,0},{2,1},{3,2},{4,7},{5,4},{6,5},{7,6},{8,11},{9,8},{10,9... | collective-permute-start | bytes 19208 | tf_op jit(solution)/shard_map/ppermute | solution.py:11
  118.4 9.4 %collective-permute-start.15 = (f32[600,64]{1,0:T(8,128)S(1)}, f32[600,64]{1,0:T(8,128)S(1)}, u32[]{:S(2)}, u32[]{:S(2)}) collective-permute-start(f32[600,64]{1,0:T(8,128)S(1)} %get-tuple-element.125), channel_id=1, source_target_pairs={{0,1},{1,2},{2,3},{3,0},{4,5},{5,6},{6,7},{7,4},{8,9},{9,10},{10,1... | collective-permute-start | bytes 460808 | tf_op jit(solution)/shard_map/ppermute | solution.py:11
  119.7 73.5 %collective-permute-start.40 = (f32[25,64]{1,0:T(8,128)}, f32[25,64]{1,0:T(8,128)S(1)}, u32[]{:S(2)}, u32[]{:S(2)}) collective-permute-start(f32[25,64]{1,0:T(8,128)} %convolution_bitcast_fusion.16), channel_id=1, source_target_pairs={{0,4},{4,8},{8,12},{12,16},{16,20},{20,24},{24,28},{28,0},{1,5},{5... | collective-permute-start | bytes 19208 | tf_op jit(solution)/shard_map/ppermute | solution.py:11
  123.0 13.5 %collective-permute-start.13 = (f32[600,64]{1,0:T(8,128)S(1)}, f32[600,64]{1,0:T(8,128)S(1)}, u32[]{:S(2)}, u32[]{:S(2)}) collective-permute-start(f32[600,64]{1,0:T(8,128)S(1)} %get-tuple-element.127), channel_id=1, source_target_pairs={{0,4},{4,8},{8,12},{12,16},{16,20},{20,24},{24,28},{28,0},{1,5},{5... | collective-permute-start | bytes 460808 | tf_op jit(solution)/shard_map/ppermute | solution.py:11
  123.0 16.1 %collective-permute-start.12 = (f32[600,64]{1,0:T(8,128)S(1)}, f32[600,64]{1,0:T(8,128)S(1)}, u32[]{:S(2)}, u32[]{:S(2)}) collective-permute-start(f32[600,64]{1,0:T(8,128)S(1)} %get-tuple-element.124), channel_id=1, source_target_pairs={{0,28},{4,0},{8,4},{12,8},{16,12},{20,16},{24,20},{28,24},{1,29},{... | collective-permute-start | bytes 460808 | tf_op jit(solution)/shard_map/ppermute | solution.py:11
  143.1 13.4 %collective-permute-start.16 = (f32[600,64]{1,0:T(8,128)S(1)}, f32[600,64]{1,0:T(8,128)S(1)}, u32[]{:S(2)}, u32[]{:S(2)}) collective-permute-start(f32[600,64]{1,0:T(8,128)S(1)} %fusion.49), channel_id=1, source_target_pairs={{0,4},{4,8},{8,12},{12,16},{16,20},{20,24},{24,28},{28,0},{1,5},{5... | collective-permute-start | bytes 460808 | tf_op jit(solution)/shard_map/ppermute | solution.py:11
  143.7 19.0 %collective-permute-start.17 = (f32[600,64]{1,0:T(8,128)S(1)}, f32[600,64]{1,0:T(8,128)S(1)}, u32[]{:S(2)}, u32[]{:S(2)}) collective-permute-start(f32[600,64]{1,0:T(8,128)S(1)} %fusion.55), channel_id=1, source_target_pairs={{0,28},{4,0},{8,4},{12,8},{16,12},{20,16},{24,20},{28,24},{1,29},{... | collective-permute-start | bytes 460808 | tf_op jit(solution)/shard_map/ppermute | solution.py:11
  147.9 14.8 %collective-permute-start.18 = (f32[600,64]{1,0:T(8,128)S(1)}, f32[600,64]{1,0:T(8,128)S(1)}, u32[]{:S(2)}, u32[]{:S(2)}) collective-permute-start(f32[600,64]{1,0:T(8,128)S(1)} %fusion.61), channel_id=1, source_target_pairs={{0,1},{1,2},{2,3},{3,0},{4,5},{5,6},{6,7},{7,4},{8,9},{9,10},{10,1... | collective-permute-start | bytes 460808 | tf_op jit(solution)/shard_map/ppermute | solution.py:11
  147.9 16.5 %collective-permute-start.19 = (f32[600,64]{1,0:T(8,128)S(1)}, f32[600,64]{1,0:T(8,128)S(1)}, u32[]{:S(2)}, u32[]{:S(2)}) collective-permute-start(f32[600,64]{1,0:T(8,128)S(1)} %fusion.67), channel_id=1, source_target_pairs={{0,3},{1,0},{2,1},{3,2},{4,7},{5,4},{6,5},{7,6},{8,11},{9,8},{10,9... | collective-permute-start | bytes 460808 | tf_op jit(solution)/shard_map/ppermute | solution.py:11
  156.5 36.7 %collective-permute-start.41 = (f32[25,64]{1,0:T(8,128)}, f32[25,64]{1,0:T(8,128)S(1)}, u32[]{:S(2)}, u32[]{:S(2)}) collective-permute-start(f32[25,64]{1,0:T(8,128)} %convolution_bitcast_fusion.15), channel_id=1, source_target_pairs={{0,28},{4,0},{8,4},{12,8},{16,12},{20,16},{24,20},{28,24},{1,29},{... | collective-permute-start | bytes 19208 | tf_op jit(solution)/shard_map/ppermute | solution.py:11
  162.7 30.5 %collective-permute-start.42 = (f32[25,64]{1,0:T(8,128)}, f32[25,64]{1,0:T(8,128)S(1)}, u32[]{:S(2)}, u32[]{:S(2)}) collective-permute-start(f32[25,64]{1,0:T(8,128)} %convolution_bitcast_fusion.14), channel_id=1, source_target_pairs={{0,1},{1,2},{2,3},{3,0},{4,5},{5,6},{6,7},{7,4},{8,9},{9,10},{10,1... | collective-permute-start | bytes 19208 | tf_op jit(solution)/shard_map/ppermute | solution.py:11
  162.7 30.5 %collective-permute-start.43 = (f32[25,64]{1,0:T(8,128)}, f32[25,64]{1,0:T(8,128)}, u32[]{:S(2)}, u32[]{:S(2)}) collective-permute-start(f32[25,64]{1,0:T(8,128)} %convolution_bitcast_fusion.13), channel_id=1, source_target_pairs={{0,3},{1,0},{2,1},{3,2},{4,7},{5,4},{6,5},{7,6},{8,11},{9,8},{10,9... | collective-permute-start | bytes 19208 | tf_op jit(solution)/shard_map/ppermute | solution.py:11
  195.8 11.9 %collective-permute-start.29 = (f32[600,64]{1,0:T(8,128)S(1)}, f32[600,64]{1,0:T(8,128)S(1)}, u32[]{:S(2)}, u32[]{:S(2)}) collective-permute-start(f32[600,64]{1,0:T(8,128)S(1)} %get-tuple-element.123), channel_id=1, source_target_pairs={{0,4},{4,8},{8,12},{12,16},{16,20},{20,24},{24,28},{28,0},{1,5},{5... | collective-permute-start | bytes 460808 | tf_op jit(solution)/shard_map/ppermute | solution.py:11
  195.8 14.6 %collective-permute-start.28 = (f32[600,64]{1,0:T(8,128)S(1)}, f32[600,64]{1,0:T(8,128)S(1)}, u32[]{:S(2)}, u32[]{:S(2)}) collective-permute-start(f32[600,64]{1,0:T(8,128)S(1)} %get-tuple-element.120), channel_id=1, source_target_pairs={{0,28},{4,0},{8,4},{12,8},{16,12},{20,16},{24,20},{28,24},{1,29},{... | collective-permute-start | bytes 460808 | tf_op jit(solution)/shard_map/ppermute | solution.py:11
  214.3 13.9 %collective-permute-start.32 = (f32[600,64]{1,0:T(8,128)S(1)}, f32[600,64]{1,0:T(8,128)S(1)}, u32[]{:S(2)}, u32[]{:S(2)}) collective-permute-start(f32[600,64]{1,0:T(8,128)S(1)} %fusion.72), channel_id=1, source_target_pairs={{0,4},{4,8},{8,12},{12,16},{16,20},{20,24},{24,28},{28,0},{1,5},{5... | collective-permute-start | bytes 460808 | tf_op jit(solution)/shard_map/ppermute | solution.py:11
  214.9 15.5 %collective-permute-start.33 = (f32[600,64]{1,0:T(8,128)S(1)}, f32[600,64]{1,0:T(8,128)S(1)}, u32[]{:S(2)}, u32[]{:S(2)}) collective-permute-start(f32[600,64]{1,0:T(8,128)S(1)} %fusion.78), channel_id=1, source_target_pairs={{0,28},{4,0},{8,4},{12,8},{16,12},{20,16},{24,20},{28,24},{1,29},{... | collective-permute-start | bytes 460808 | tf_op jit(solution)/shard_map/ppermute | solution.py:11
  219.1 11.3 %collective-permute-start.34 = (f32[600,64]{1,0:T(8,128)S(1)}, f32[600,64]{1,0:T(8,128)S(1)}, u32[]{:S(2)}, u32[]{:S(2)}) collective-permute-start(f32[600,64]{1,0:T(8,128)S(1)} %fusion.84), channel_id=1, source_target_pairs={{0,1},{1,2},{2,3},{3,0},{4,5},{5,6},{6,7},{7,4},{8,9},{9,10},{10,1... | collective-permute-start | bytes 460808 | tf_op jit(solution)/shard_map/ppermute | solution.py:11
  219.1 11.3 %collective-permute-start.35 = (f32[600,64]{1,0:T(8,128)S(1)}, f32[600,64]{1,0:T(8,128)S(1)}, u32[]{:S(2)}, u32[]{:S(2)}) collective-permute-start(f32[600,64]{1,0:T(8,128)S(1)} %fusion.90), channel_id=1, source_target_pairs={{0,3},{1,0},{2,1},{3,2},{4,7},{5,4},{6,5},{7,6},{8,11},{9,8},{10,9... | collective-permute-start | bytes 460808 | tf_op jit(solution)/shard_map/ppermute | solution.py:11
  260.3 13.7 %collective-permute-start.45 = (f32[600,64]{1,0:T(8,128)S(1)}, f32[600,64]{1,0:T(8,128)S(1)}, u32[]{:S(2)}, u32[]{:S(2)}) collective-permute-start(f32[600,64]{1,0:T(8,128)S(1)} %get-tuple-element.119), channel_id=1, source_target_pairs={{0,4},{4,8},{8,12},{12,16},{16,20},{20,24},{24,28},{28,0},{1,5},{5... | collective-permute-start | bytes 460808 | tf_op jit(solution)/shard_map/ppermute | solution.py:11
  260.7 15.5 %collective-permute-start.44 = (f32[600,64]{1,0:T(8,128)S(1)}, f32[600,64]{1,0:T(8,128)S(1)}, u32[]{:S(2)}, u32[]{:S(2)}) collective-permute-start(f32[600,64]{1,0:T(8,128)S(1)} %get-tuple-element.116), channel_id=1, source_target_pairs={{0,28},{4,0},{8,4},{12,8},{16,12},{20,16},{24,20},{28,24},{1,29},{... | collective-permute-start | bytes 460808 | tf_op jit(solution)/shard_map/ppermute | solution.py:11
  (133 other events, 1008.4 us)
where the time goes:
time: 281 us; the launch traced here: 278 us
  matrix products  91.4 us (33%)
  starting transfers between devices  77.9 us (28%)
  waiting for transfers between devices  42.3 us (15%)
  other arithmetic  36.4 us (13%)
  local copies, waits for them, and re-layouts  28 us (10%)
    ppermute x48, starting transfers between devices, from_behind(): return lax.ppermute(x, axis, [(i, (i + by) % peers) for i in range(peers)])  77.9 us
    ppermute x48, waiting for transfers between devices, from_behind(): return lax.ppermute(x, axis, [(i, (i + by) % peers) for i in range(peers)])  42.3 us
    dot_general x57, matrix products, select_dot(): jnp.dot(left, right, precision=HIGHEST, preferred_element_type=jnp.float32)  35.2 us
    dot_general x9, matrix products, derivative(): jnp.einsum('qb,fbs->fqs', basis_quad, values, precision=HIGHEST, preferre...  25.6 us
    dot_general x9, matrix products, derivative(): jnp.einsum('bq,gqs->gbs', test_deriv, flux_all, precision=HIGHEST, prefer...  21.1 us
    unnamed x36, other arithmetic  20.1 us
    dot_general x9, matrix products, trace_values(): jnp.einsum('b,fbs->fs', trace_vec, values, precision=HIGHEST, preferred_e...  9.52 us
    concatenate x3, local copies, waits for them, and re-layouts, per_device(): jnp.concatenate([payload_flat * keep[None, :]] + [piece[0] for piece in i...  8.26 us
  transfers between devices with their start and end apart: 48, of which 12 were waited for; matrix products, arithmetic and copies ran while one was open for 41% of the time, Pallas kernels for 0%

commit v1 on v0

v1 whole, which is shorter than its diff:
```python
import functools

import jax
import jax.numpy as jnp
from jax import lax
from jax.experimental import pallas as pl
from jax.experimental.pallas import tpu as pltpu
from jax.sharding import PartitionSpec as P

F32 = jnp.float32
BF16 = jnp.bfloat16
HIGHEST = lax.Precision.HIGHEST
MESH = pl.DeviceIdType.MESH
SCALE = 8.0
ROWS = 16
LANES = 128


def up(n, m):
    return -(-n // m) * m


def dot32(a, b):
    return jnp.dot(a, b, precision=HIGHEST, preferred_element_type=F32)


def split2(x):
    hi = x.astype(BF16)
    lo = (x - hi.astype(F32)).astype(BF16)
    return hi, lo


def split3(x):
    hi = x.astype(BF16)
    rest = x - hi.astype(F32)
    mid = rest.astype(BF16)
    lo = (rest - mid.astype(F32)).astype(BF16)
    return jnp.concatenate([hi, mid, lo], axis=0)


def fold3(x):
    n = x.shape[0] // 3
    return x[:n] + (x[n : 2 * n] + x[2 * n :])


def seg_sum(x, onehot):
    return fold3(
        lax.dot_general(
            split3(x), onehot, (((1,), (1,)), ((), ())), preferred_element_type=F32
        )
    )


def seg_take(x, onehot):
    return fold3(jnp.dot(split3(x), onehot, preferred_element_type=F32))


def kernel(
    sizes,
    state_ref,
    coef_ref,
    bq_ref,
    td_ref,
    trace_ref,
    lift_ref,
    height_ref,
    tent_ref,
    out_ref,
    hot_ref,
    lhs_ref,
    cs_ref,
    mom_ref,
    x_ref,
    d_ref,
    cur_ref,
    g_ref,
    stat_ref,
    stat_in,
    part_ref,
    part_in,
    tot_ref,
    tot_in,
    send_sem,
    recv_sem,
):
    n_first, n_second = sizes
    fields, basis, n_elem = state_ref.shape
    levels, tent_dev = height_ref.shape
    pair = 2 * tent_dev
    wide = up(basis, LANES)
    crows = cs_ref.shape[0]
    me_first = lax.axis_index("gx")
    me_second = lax.axis_index("gy")
    next_first = lax.rem(me_first + 1, n_first)
    prev_first = lax.rem(me_first + n_first - 1, n_first)
    next_second = lax.rem(me_second + 1, n_second)
    prev_second = lax.rem(me_second + n_second - 1, n_second)
    peers = [
        (next_first, me_second),
        (prev_first, me_second),
        (me_first, next_second),
        (me_first, prev_second),
    ]

    barrier = pltpu.get_barrier_semaphore()
    for peer in peers:
        pl.semaphore_signal(barrier, inc=1, device_id=peer, device_id_type=MESH)

    def remote(src, dst, slot, k):
        return pltpu.make_async_remote_copy(
            src_ref=src,
            dst_ref=dst,
            send_sem=send_sem.at[slot, k],
            recv_sem=recv_sem.at[slot, k],
            device_id=peers[k],
            device_id_type=MESH,
        )

    cs_ref[...] = jnp.zeros_like(cs_ref)
    for g in range(fields):
        cs_ref[g * fields : (g + 1) * fields, :] = coef_ref[g]
    cs_ref[fields * fields : fields * fields + 1, :] = jnp.ones((1, n_elem), F32)
    for level in range(levels):
        tents = tent_ref[level : level + 1, :]
        owner = tents // tent_dev
        local = tents - owner * tent_dev
        own_first = owner // n_second
        own_second = owner - own_first * n_second
        base = jnp.where(
            own_first == me_first,
            jnp.where(
                own_second == me_second,
                0,
                jnp.where(own_second == next_second, 2 * pair, 2 * pair + tent_dev),
            ),
            jnp.where(own_first == next_first, pair, pair + tent_dev),
        )
        column = base + local
        rows = lax.broadcasted_iota(jnp.int32, (3 * pair, n_elem), 0)
        hot_ref[level] = jnp.where(rows == column, 1.0, 0.0).astype(F32).astype(BF16)

    stat_ref[...] = jnp.zeros_like(stat_ref)
    for level in range(levels):
        sums = seg_sum(cs_ref[...], hot_ref[level])
        for block in range(3):
            stat_ref[block, level * crows : (level + 1) * crows, :] = sums[
                :, block * pair : (block + 1) * pair
            ]
    hrow = levels * crows
    for block in range(3):
        stat_ref[block, hrow : hrow + levels, 0:tent_dev] = SCALE * height_ref[...]
    pl.semaphore_wait(barrier, 4)
    stat_copies = [
        remote(stat_ref.at[1 + k // 2], stat_in.at[k], 0, k) for k in range(4)
    ]
    for copy in stat_copies:
        copy.start()

    a = dot32(td_ref[...] * (1.0 / SCALE), bq_ref[...])
    a2 = dot32(a, a)
    a4 = dot32(a2, a2)
    lift_row = lift_ref[...] * (1.0 / SCALE)
    r0 = trace_ref[...]
    r1 = dot32(r0, a)
    r01 = jnp.concatenate([r0, r1], axis=0)
    r23 = dot32(r01, a2)
    r03 = jnp.concatenate([r01, r23], axis=0)
    r47 = dot32(r03, a4)
    r8 = dot32(r47[3:4], a)
    powers = jnp.concatenate(
        [r03, r47, r8, jnp.zeros((ROWS - 9, basis), F32)], axis=0
    )
    tau = jnp.sum(powers * lift_row, axis=1, keepdims=True)
    tau1 = tau[1:2]

    p_hi, p_lo = split2(powers)
    p_all = jnp.concatenate([p_hi, p_lo], axis=0)
    for f in range(fields):
        s_hi, s_lo = split2(state_ref[f])
        both = jnp.dot(p_all, s_hi, preferred_element_type=F32)
        rest = jnp.dot(p_hi, s_lo, preferred_element_type=F32)
        mom_ref[f] = both[:ROWS] + (both[ROWS:] + rest)

    eye = lax.broadcasted_iota(jnp.int32, (basis, basis), 0) == (
        lax.broadcasted_iota(jnp.int32, (basis, basis), 1)
    )
    lift_col = jnp.sum(jnp.where(eye, lift_row, 0.0), axis=1, keepdims=True)
    cur_ref[...] = jnp.zeros_like(cur_ref)
    cur_ref[0, :, 0:basis] = a
    cur_ref[0, :, basis : basis + 1] = lift_col
    a_hi, a_lo = split2(
        jnp.concatenate(
            [cur_ref[0, :, 0:wide], jnp.zeros((wide - basis, wide), F32)], axis=0
        )
    )
    lhs_ref[...] = jnp.concatenate(
        [
            jnp.concatenate([a_hi, a_hi], axis=1),
            jnp.concatenate([a_lo, a_lo], axis=1),
        ],
        axis=0,
    )

    def coef_row(g, f):
        return coef_ref[g, f : f + 1, :]

    def mix(values):
        result = []
        for g in range(fields):
            total = coef_row(g, 0) * values[0]
            for f in range(1, fields):
                total = total + coef_row(g, f) * values[f]
            result.append(total)
        return result

    def shift(values):
        return [pltpu.roll(v, ROWS - 1, 0) for v in values]

    chunk = g_ref.shape[2]

    def advance(level, part):
        lo_lane = part * chunk
        lanes = slice(lo_lane, lo_lane + chunk)
        source = state_ref if level == 0 else out_ref
        h = d_ref[level, 3 * fields : 3 * fields + 1, lanes]
        weights = [h, h * h * 0.5, h * h * h * (1.0 / 6.0)]
        for section in range(3):
            for tile in range(chunk // LANES):
                at = slice(lo_lane + tile * LANES, lo_lane + (tile + 1) * LANES)
                here = slice(tile * LANES, (tile + 1) * LANES)
                bc = [
                    [
                        jnp.broadcast_to(coef_ref[g, f : f + 1, at], (16, LANES))
                        for f in range(fields)
                    ]
                    for g in range(fields)
                ]
                first = lax.broadcasted_iota(jnp.int32, (wide - basis, LANES), 0) == 0
                for row in range(0, wide, 16):
                    size = min(16, basis - row)
                    if section == 0:
                        v = [source[f, row : row + size, at] for f in range(fields)]
                    else:
                        v = [cur_ref[f, row : row + size, here] for f in range(fields)]
                    for g in range(fields):
                        total = bc[g][0][:size] * v[0]
                        for f in range(1, fields):
                            total = total + bc[g][f][:size] * v[f]
                        if size < 16:
                            drow = section * fields + g
                            tail = jnp.where(
                                first, d_ref[level, drow : drow + 1, at], 0.0
                            )
                            total = jnp.concatenate([total, tail], axis=0)
                        hi, lo = split2(total)
                        g_ref[g, row : row + 16, here] = hi
                        g_ref[g, wide + row : wide + row + 16, here] = lo
            for g in range(fields):
                res = jnp.dot(lhs_ref[...], g_ref[g], preferred_element_type=F32)
                deriv = res[:basis] + res[wide : wide + basis]
                if section < 2:
                    cur_ref[g] = deriv
                prior = source[g, :, lanes] if section == 0 else out_ref[g, :, lanes]
                out_ref[g, :, lanes] = prior + weights[section] * deriv

    lane = lax.broadcasted_iota(jnp.int32, (ROWS, pair), 1)
    copies = list(stat_copies)
    parts = n_elem // chunk
    for level in range(levels):
        moments = [mom_ref[f] for f in range(fields)]
        lead = mix(shift(moments))
        for f in range(fields):
            x_ref[f : f + 1, :] = moments[f][0:1]
            x_ref[fields + f : fields + f + 1, :] = lead[f][0:1]
        inner = [lead[f][1:2] - tau1 * moments[f][0:1] for f in range(fields)]
        for g, value in enumerate(mix(inner)):
            x_ref[2 * fields + g : 2 * fields + g + 1, :] = value
        x_ref[3 * fields : ROWS, :] = jnp.zeros((ROWS - 3 * fields, n_elem), F32)
        sums = seg_sum(x_ref[...], hot_ref[level])
        for block in range(2):
            part_ref[level, block] = sums[:, (1 + block) * pair : (2 + block) * pair]
        going = [
            remote(part_ref.at[level, k // 2], part_in.at[level, k], 1 + level, k)
            for k in range(4)
        ]
        for copy in going:
            copy.start()
        if level > 0:
            for part in range(parts // 2):
                advance(level - 1, part)
        if level == 0:
            for copy in stat_copies:
                copy.wait_recv()
        for copy in going:
            copy.wait_recv()
        own = sums[:, :pair]
        own = own + part_in[level, 0] + part_in[level, 2]
        own = own + pltpu.roll(part_in[level, 1] + part_in[level, 3], tent_dev, 1)
        srows = slice(level * crows, (level + 1) * crows)
        stat = stat_ref[0, srows] + stat_in[0, srows] + stat_in[2, srows]
        stat = stat + pltpu.roll(stat_in[1, srows] + stat_in[3, srows], tent_dev, 1)
        count = jnp.maximum(stat[fields * fields : fields * fields + 1], 1.0)
        mean0 = [own[f : f + 1] / count for f in range(fields)]
        for f in range(fields):
            tot_ref[level, f : f + 1, :] = mean0[f]
            tot_ref[level, fields + f : fields + f + 1, :] = (
                own[fields + f : fields + f + 1] / count
            )
            joint = stat[f * fields : f * fields + 1] * mean0[0]
            for s in range(1, fields):
                joint = joint + stat[f * fields + s : f * fields + s + 1] * mean0[s]
            row = 2 * fields + f
            tot_ref[level, row : row + 1, :] = (
                own[row : row + 1] + tau1 * joint
            ) / count
        tot_ref[level, 3 * fields : ROWS, :] = jnp.broadcast_to(
            stat_ref[0, hrow + level : hrow + level + 1], (ROWS - 3 * fields, pair)
        )
        back = [
            remote(tot_ref.at[level], tot_in.at[level, k], 1 + levels + level, k)
            for k in range(4)
        ]
        for copy in back:
            copy.start()
        copies += going + back
        if level > 0:
            for part in range(parts // 2, parts):
                advance(level - 1, part)
        for copy in back:
            copy.wait_recv()
        low = lane < tent_dev
        table = jnp.concatenate(
            [
                tot_ref[level],
                jnp.where(low, tot_in[level, 1], pltpu.roll(tot_in[level, 0], tent_dev, 1)),
                jnp.where(low, tot_in[level, 3], pltpu.roll(tot_in[level, 2], tent_dev, 1)),
            ],
            axis=1,
        )
        each = seg_take(table, hot_ref[level])
        h = each[3 * fields : 3 * fields + 1]
        d_ref[level, 3 * fields : ROWS, :] = each[3 * fields : ROWS]
        d0 = [each[f : f + 1] - moments[f][0:1] for f in range(fields)]
        n1 = [lead[f] + tau * d0[f] for f in range(fields)]
        d1 = [each[fields + f : fields + f + 1] - n1[f][0:1] for f in range(fields)]
        n2 = mix(shift(n1))
        n2 = [n2[f] + tau * d1[f] for f in range(fields)]
        d2 = [
            each[2 * fields + f : 2 * fields + f + 1] - n2[f][0:1]
            for f in range(fields)
        ]
        for f in range(fields):
            d_ref[level, f : f + 1, :] = d0[f]
            d_ref[level, fields + f : fields + f + 1, :] = d1[f]
            d_ref[level, 2 * fields + f : 2 * fields + f + 1, :] = d2[f]
        if level < levels - 1:
            n3 = mix(shift(n2))
            for f in range(fields):
                third = n3[f] + tau * d2[f]
                mom_ref[f] = moments[f] + h * (
                    n1[f] + (h * 0.5) * (n2[f] + (h * (1.0 / 3.0)) * third)
                )
    for part in range(parts):
        advance(levels - 1, part)
    for copy in copies:
        copy.wait_send()


def per_device(
    sizes, state, coef, basis_quad, test_deriv, trace_vec, lift_vec, tent_height, elem_tent
):
    fields, basis, n_elem = state.shape
    levels, tent_dev = tent_height.shape
    pair = 2 * tent_dev
    wide = up(basis, LANES)
    crows = up(fields * fields + 1, 8)
    srows = up(levels * crows + levels, 8)
    chunk = min(256, n_elem)
    vmem = pl.BlockSpec(memory_space=pltpu.VMEM)
    return pl.pallas_call(
        functools.partial(kernel, sizes),
        out_shape=jax.ShapeDtypeStruct(state.shape, F32),
        in_specs=[vmem] * 8,
        out_specs=vmem,
        scratch_shapes=[
            pltpu.VMEM((levels, 3 * pair, n_elem), BF16),
            pltpu.VMEM((2 * wide, 2 * wide), BF16),
            pltpu.VMEM((crows, n_elem), F32),
            pltpu.VMEM((fields, ROWS, n_elem), F32),
            pltpu.VMEM((ROWS, n_elem), F32),
            pltpu.VMEM((levels, ROWS, n_elem), F32),
            pltpu.VMEM((fields, basis, chunk), F32),
            pltpu.VMEM((fields, 2 * wide, chunk), BF16),
            pltpu.VMEM((3, srows, pair), F32),
            pltpu.VMEM((4, srows, pair), F32),
            pltpu.VMEM((levels, 2, ROWS, pair), F32),
            pltpu.VMEM((levels, 4, ROWS, pair), F32),
            pltpu.VMEM((levels, ROWS, pair), F32),
            pltpu.VMEM((levels, 4, ROWS, pair), F32),
            pltpu.SemaphoreType.DMA((1 + 2 * levels, 4)),
            pltpu.SemaphoreType.DMA((1 + 2 * levels, 4)),
        ],
        compiler_params=pltpu.CompilerParams(
            collective_id=0, has_side_effects=True, vmem_limit_bytes=40 * 1024 * 1024
        ),
    )(
        state,
        coef,
        basis_quad,
        test_deriv,
        trace_vec.reshape(1, basis),
        lift_vec.reshape(1, basis),
        tent_height,
        elem_tent,
    )


def solution(mesh):
    split = ("gx", "gy")
    placed = (
        P(None, None, split),
        P(None, None, split),
        P(),
        P(),
        P(),
        P(),
        P(None, split),
        P(None, split),
    )
    sizes = (mesh.shape["gx"], mesh.shape["gy"])
    return jax.shard_map(
        functools.partial(per_device, sizes),
        mesh=mesh,
        in_specs=placed,
        out_specs=P(None, None, split),
        check_vma=False,
    )
```

time: 281 us -> 45.9 us (0.16)
  matrix products: 91.4 us -> 0 us
  starting transfers between devices: 77.9 us -> 0 us
  waiting for transfers between devices: 42.3 us -> 0 us
  Pallas kernels: 0 us -> 37.8 us
  other arithmetic: 36.4 us -> 0 us
  local copies, waits for them, and re-layouts: 28 us -> 7.77 us
    dot_general x84 -> x0, matrix products: 91.4 us -> none  [the longest x57 35.2 us: select_dot(): jnp.dot(left, right, precision=HIGHEST, preferred_element_type=jnp.float32)]
    ppermute x48 -> x0, starting transfers between devices: 77.9 us -> none  [from_behind(): return lax.ppermute(x, axis, [(i, (i + by) % peers) for i in range(peers)])]
    ppermute x48 -> x0, waiting for transfers between devices: 42.3 us -> none  [from_behind(): return lax.ppermute(x, axis, [(i, (i + by) % peers) for i in range(peers)])]
    pallas_call x0 -> x1, Pallas kernels: none -> 37.8 us  [per_device(): pl.pallas_call(functools.partial(kernel, sizes), out_shape=jax.ShapeDtype...]
    unnamed x36 -> x0, other arithmetic: 20.1 us -> none
    concatenate x21 -> x0, local copies, waits for them, and re-layouts: 11.6 us -> none  [the longest x3 8.26 us: per_device(): jnp.concatenate([payload_flat * keep[None, :]] + [piece[0] for piece in i...]
    another operation x33 -> x0, other arithmetic: 6.41 us -> none
    ppermute x4 -> x0, local copies, waits for them, and re-layouts: 3.49 us -> none  [from_behind(): return lax.ppermute(x, axis, [(i, (i + by) % peers) for i in range(peers)])]
  transfers between devices with their start and end apart: 48 -> 0, of which waited for: 12 -> 0; matrix products, arithmetic and copies ran while one was open for 41% -> 0% of each run, Pallas kernels for 0% -> 0%
where the time goes in v1:
time: 45.9 us; the launch traced here: 45.6 us
  Pallas kernels  37.8 us (82%)
  local copies, waits for them, and re-layouts  7.77 us (17%)
    pallas_call x1, Pallas kernels, per_device(): pl.pallas_call(functools.partial(kernel, sizes), out_shape=jax.ShapeDtype...  37.8 us
    unnamed x16, local copies, waits for them, and re-layouts  7.77 us

profile of v1, /device:TPU:0, one launch (start us, length us, event | category | flops | bytes accessed | tf_op | source)
XLA Modules:
  0.0 45.6 jit_solution(3710899336806971623)
XLA Ops:
  0.0 1.0 %copy.9.td_ref = f32[120,216]{1,0:T(8,128)S(1)} copy(f32[120,216]{0,1:T(8,128)} %param.11) | data formatting | bytes 207360 | tf_op args[3]
  1.0 0.0 copy-start
  1.0 1.3 %copy-done = f32[5,120,512]{2,1,0:T(8,128)S(1)} copy-done((f32[5,120,512]{2,1,0:T(8,128)S(1)}, f32[5,120,512]{2,1,0:T(8,128)}, u32[]{:S(2)}) %copy-start) | copy-done | bytes 1228824
  2.3 0.0 copy-start.1
  2.3 0.9 %copy-done.1 = f32[216,120]{1,0:T(8,128)S(1)} copy-done((f32[216,120]{1,0:T(8,128)S(1)}, f32[216,120]{1,0:T(8,128)}, u32[]{:S(2)}) %copy-start.1) | copy-done | bytes 103704
  3.2 0.0 copy-start.2
  3.2 0.9 %copy-done.2 = f32[5,5,512]{2,1,0:T(8,128)S(1)} copy-done((f32[5,5,512]{2,1,0:T(8,128)S(1)}, f32[5,5,512]{2,1,0:T(8,128)}, u32[]{:S(2)}) %copy-start.2) | copy-done | bytes 51224
  4.1 0.0 copy-start.3
  4.1 0.7 %copy-done.3 = s32[3,512]{1,0:T(4,128)S(1)} copy-done((s32[3,512]{1,0:T(4,128)S(1)}, s32[3,512]{1,0:T(4,128)}, u32[]{:S(2)}) %copy-start.3) | copy-done | bytes 6168
  4.8 0.0 copy-start.4
  4.8 0.7 %copy-done.4 = f32[3,64]{1,0:T(4,128)S(1)} copy-done((f32[3,64]{1,0:T(4,128)S(1)}, f32[3,64]{1,0:T(4,128)}, u32[]{:S(2)}) %copy-start.4) | copy-done | bytes 792
  5.5 0.0 copy-start.5
  5.5 0.7 %copy-done.5 = f32[120]{0:T(128)S(1)} copy-done((f32[120]{0:T(128)S(1)}, f32[120]{0:T(128)}, u32[]{:S(2)}) %copy-start.5) | copy-done | bytes 504
  6.1 0.0 copy-start.6
  6.1 0.7 %copy-done.6 = f32[120]{0:T(128)S(1)} copy-done((f32[120]{0:T(128)S(1)}, f32[120]{0:T(128)}, u32[]{:S(2)}) %copy-start.6) | copy-done | bytes 504
  6.8 37.8 %shard_map.82 = f32[5,120,512]{2,1,0:T(8,128)S(1)} custom-call(f32[5,120,512]{2,1,0:T(8,128)S(1)} %copy-done, f32[5,5,512]{2,1,0:T(8,128)S(1)} %copy-done.2, f32[216,120]{1,0:T(8,128)S(1)} %copy-done.1, f32[120,216]{1,0:T(8,128)S(1)} %copy.9.td_ref, f32[1,120]{1,0:T(1,128)S(1)} %bitcast.2, f32[1,120]{1,0:T(1,128)S(1)} %bitcast.3, f32[3,64]{1,0:T(4,128)S(1)} %copy-done.4, ...), custom_call_target="tpu_custom_call" | custom-call | tf_op jit(solution)/shard_map/pallas_call | solution.py:380
  44.5 1.0 %copy.11 = f32[5,120,512]{2,1,0:T(8,128)} copy(f32[5,120,512]{2,1,0:T(8,128)S(1)} %shard_map.82) | data formatting | bytes 2457600
Async XLA Ops:
  1.0 1.3 %copy-start = (f32[5,120,512]{2,1,0:T(8,128)S(1)}, f32[5,120,512]{2,1,0:T(8,128)}, u32[]{:S(2)}) copy-start(f32[5,120,512]{2,1,0:T(8,128)} %state_ref.1) | copy-start | bytes 3686404
  2.3 0.9 %copy-start.1 = (f32[216,120]{1,0:T(8,128)S(1)}, f32[216,120]{1,0:T(8,128)}, u32[]{:S(2)}) copy-start(f32[216,120]{1,0:T(8,128)} %bq_ref.1) | copy-start | bytes 311044
  3.2 0.9 %copy-start.2 = (f32[5,5,512]{2,1,0:T(8,128)S(1)}, f32[5,5,512]{2,1,0:T(8,128)}, u32[]{:S(2)}) copy-start(f32[5,5,512]{2,1,0:T(8,128)} %coef_ref.1) | copy-start | bytes 153604
  4.1 0.7 %copy-start.3 = (s32[3,512]{1,0:T(4,128)S(1)}, s32[3,512]{1,0:T(4,128)}, u32[]{:S(2)}) copy-start(s32[3,512]{1,0:T(4,128)} %tent_ref.1) | copy-start | bytes 18436
  4.8 0.7 %copy-start.4 = (f32[3,64]{1,0:T(4,128)S(1)}, f32[3,64]{1,0:T(4,128)}, u32[]{:S(2)}) copy-start(f32[3,64]{1,0:T(4,128)} %height_ref.1) | copy-start | bytes 2308
  5.5 0.7 %copy-start.5 = (f32[120]{0:T(128)S(1)}, f32[120]{0:T(128)}, u32[]{:S(2)}) copy-start(f32[120]{0:T(128)} %param.12) | copy-start | bytes 1444
  6.1 0.7 %copy-start.6 = (f32[120]{0:T(128)S(1)}, f32[120]{0:T(128)}, u32[]{:S(2)}) copy-start(f32[120]{0:T(128)} %param.13) | copy-start | bytes 1444

commit v2 on v1

v2 whole, which is shorter than its diff:
```python
import functools

import jax
import jax.numpy as jnp
from jax import lax
from jax.experimental import pallas as pl
from jax.experimental.pallas import tpu as pltpu
from jax.sharding import PartitionSpec as P

F32 = jnp.float32
BF16 = jnp.bfloat16
MESH = pl.DeviceIdType.MESH
SCALE = 8.0
GROUP = 8
POWERS = 9
LANES = 128


def up(n, m):
    return -(-n // m) * m


NN = (((1,), (0,)), ((), ()))
NT = (((1,), (1,)), ((), ()))
TN = (((0,), (0,)), ((), ()))


def dot3(a, b, dims=NN):
    a_hi, a_lo = split2(a)
    b_hi, b_lo = split2(b)

    def one(x, y):
        return lax.dot_general(x, y, dims, preferred_element_type=F32)

    return one(a_hi, b_hi) + (one(a_hi, b_lo) + one(a_lo, b_hi))


def split2(x):
    hi = x.astype(BF16)
    lo = (x - hi.astype(F32)).astype(BF16)
    return hi, lo


def split3(x):
    hi = x.astype(BF16)
    rest = x - hi.astype(F32)
    mid = rest.astype(BF16)
    lo = (rest - mid.astype(F32)).astype(BF16)
    return jnp.concatenate([hi, mid, lo], axis=0)


def fold3(x):
    n = x.shape[0] // 3
    return x[:n] + (x[n : 2 * n] + x[2 * n :])


def seg_sum(x, onehot):
    return fold3(
        lax.dot_general(
            split3(x), onehot, (((1,), (1,)), ((), ())), preferred_element_type=F32
        )
    )


def seg_take(x, onehot):
    return fold3(jnp.dot(split3(x), onehot, preferred_element_type=F32))


def kernel(
    sizes,
    state_hbm,
    coef_hbm,
    bq_hbm,
    td_hbm,
    trace_hbm,
    lift_hbm,
    height_hbm,
    tent_hbm,
    out_ref,
    state_ref,
    coef_ref,
    bq_ref,
    td_ref,
    trace_ref,
    lift_ref,
    height_ref,
    tent_ref,
    hot_ref,
    lhs_ref,
    cs_ref,
    ct_ref,
    cube_ref,
    mom_ref,
    fin_ref,
    v1_ref,
    v2_ref,
    g_ref,
    stat_ref,
    stat_in,
    part_ref,
    part_in,
    tot_ref,
    tot_in,
    load_sem,
    send_sem,
    recv_sem,
):
    n_first, n_second = sizes
    fields, basis, n_elem = state_ref.shape
    levels, tent_dev = height_ref.shape
    pair = 2 * tent_dev
    wide = up(basis, LANES)
    crows = cs_ref.shape[0]
    me_first = lax.axis_index("gx")
    me_second = lax.axis_index("gy")
    next_first = lax.rem(me_first + 1, n_first)
    prev_first = lax.rem(me_first + n_first - 1, n_first)
    next_second = lax.rem(me_second + 1, n_second)
    prev_second = lax.rem(me_second + n_second - 1, n_second)
    peers = [
        (next_first, me_second),
        (prev_first, me_second),
        (me_first, next_second),
        (me_first, prev_second),
    ]

    barrier = pltpu.get_barrier_semaphore()
    for peer in peers:
        pl.semaphore_signal(barrier, inc=1, device_id=peer, device_id_type=MESH)
    loads = [
        pltpu.make_async_copy(src, dst, load_sem.at[i])
        for i, (src, dst) in enumerate(
            [
                (tent_hbm, tent_ref),
                (coef_hbm, coef_ref),
                (td_hbm, td_ref),
                (bq_hbm, bq_ref),
                (trace_hbm, trace_ref),
                (lift_hbm, lift_ref),
                (height_hbm, height_ref),
                (state_hbm, state_ref),
            ]
        )
    ]
    for load in loads:
        load.start()

    def remote(src, dst, slot, k):
        return pltpu.make_async_remote_copy(
            src_ref=src,
            dst_ref=dst,
            send_sem=send_sem.at[slot, k],
            recv_sem=recv_sem.at[slot, k],
            device_id=peers[k],
            device_id_type=MESH,
        )

    def build_hot(level):
        tents = tent_ref[level : level + 1, :]
        owner = tents // tent_dev
        local = tents - owner * tent_dev
        own_first = owner // n_second
        own_second = owner - own_first * n_second
        base = jnp.where(
            own_first == me_first,
            jnp.where(
                own_second == me_second,
                0,
                jnp.where(own_second == next_second, 2 * pair, 2 * pair + tent_dev),
            ),
            jnp.where(own_first == next_first, pair, pair + tent_dev),
        )
        column = base + local
        rows = lax.broadcasted_iota(jnp.int32, (3 * pair, n_elem), 0)
        hot_ref[level] = jnp.where(rows == column, 1.0, 0.0).astype(F32).astype(BF16)

    def send_stat(level):
        sums = seg_sum(cs_ref[...], hot_ref[level])
        for block in range(3):
            stat_ref[level, block, 0:crows, :] = sums[:, block * pair : (block + 1) * pair]
            stat_ref[level, block, crows:, :] = jnp.zeros(
                (stat_ref.shape[2] - crows, pair), F32
            )
            stat_ref[level, block, crows : crows + levels, 0:tent_dev] = (
                SCALE * height_ref[...]
            )
        if level == 0:
            pl.semaphore_wait(barrier, 4)
        copies = [
            remote(stat_ref.at[level, 1 + k // 2], stat_in.at[level, k], level, k)
            for k in range(4)
        ]
        for copy in copies:
            copy.start()
        return copies

    low = lax.broadcasted_iota(jnp.int32, (1, pair), 1) < tent_dev

    def table_of(own, arrived):
        return jnp.concatenate(
            [
                own,
                jnp.where(low, arrived[1], pltpu.roll(arrived[0], tent_dev, 1)),
                jnp.where(low, arrived[3], pltpu.roll(arrived[2], tent_dev, 1)),
            ],
            axis=1,
        )

    loads[0].wait()
    build_hot(0)
    loads[1].wait()
    cs_ref[...] = jnp.zeros_like(cs_ref)
    ct_ref[...] = jnp.zeros_like(ct_ref)
    for g in range(fields):
        cs_ref[g * fields : (g + 1) * fields, :] = coef_ref[g]
        for f in range(fields):
            ct_ref[f, g : g + 1, :] = coef_ref[g, f : f + 1, :]
    cs_ref[fields * fields : fields * fields + 1, :] = jnp.ones((1, n_elem), F32)
    for load in loads[2:7]:
        load.wait()
    stat_copies = [send_stat(0)]

    a = dot3(td_ref[...] * (1.0 / SCALE), bq_ref[...], TN)
    a2 = dot3(a, a)
    a3 = dot3(a2, a)
    lift_row = lift_ref[...] * (1.0 / SCALE)
    r0 = trace_ref[...]
    r1 = dot3(r0, a)
    r2 = dot3(r0, a2)
    r02 = jnp.concatenate([r0, r1, r2], axis=0)
    r35 = dot3(r02, a3)
    r68 = dot3(r35, a3)
    powers = jnp.concatenate(
        [r02, r35, r68, jnp.zeros((16 - POWERS, basis), F32)], axis=0
    )
    taus = jnp.sum(powers * lift_row, axis=1, keepdims=True)
    tau = [taus[j : j + 1] for j in range(POWERS)]

    p_hi, p_lo = split2(powers)
    p_all = jnp.concatenate([p_hi, p_lo], axis=0)
    loads[7].wait()
    mom_ref[...] = jnp.zeros_like(mom_ref)
    for f in range(fields):
        s_hi, s_lo = split2(state_ref[f])
        both = jnp.dot(p_all, s_hi, preferred_element_type=F32)
        rest = jnp.dot(p_hi, s_lo, preferred_element_type=F32)
        found = both[:16] + (both[16:] + rest)
        for j in range(POWERS):
            mom_ref[j, f : f + 1, :] = found[j : j + 1]

    def times(v):
        total = ct_ref[0] * v[0:1]
        for f in range(1, fields):
            total = total + ct_ref[f] * v[f : f + 1]
        return total

    def operator(slot, matrix):
        pad = jnp.concatenate([matrix, jnp.zeros((wide - basis, basis), F32)], axis=0)
        lhs_ref[slot] = jnp.zeros((2 * wide, 2 * wide), BF16)
        hi, lo = split2(pad)
        for at in (0, wide):
            lhs_ref[slot, 0:wide, at : at + basis] = hi
            lhs_ref[slot, wide:, at : at + basis] = lo

    def apply(slot, matrices, source, target, terms, bases):
        step = min(2 * LANES, n_elem)
        zeros = jnp.zeros((wide - basis, LANES), F32)
        for start in range(0, n_elem, step):
            for lane in range(start, start + step, LANES):
                at = slice(lane, lane + LANES)
                bc = [
                    [
                        jnp.broadcast_to(matrices(g, f, at), (16, LANES))
                        for f in range(fields)
                    ]
                    for g in range(fields)
                ]
                for row in range(0, wide, 16):
                    size = min(16, basis - row)
                    v = [source[f, row : row + size, at] for f in range(fields)]
                    for g in range(fields):
                        total = bc[g][0][:size] * v[0]
                        for f in range(1, fields):
                            total = total + bc[g][f][:size] * v[f]
                        if size < 16:
                            total = jnp.concatenate([total, zeros], axis=0)
                        hi, lo = split2(total)
                        g_ref[g, row : row + 16, at] = hi
                        g_ref[g, wide + row : wide + row + 16, at] = lo
            lanes = slice(start, start + step)
            for g in range(fields):
                res = jnp.dot(
                    lhs_ref[slot], g_ref[g, :, lanes], preferred_element_type=F32
                )
                total = res[:basis] + res[wide : wide + basis]
                for term, base in zip(terms, bases):
                    value = base[g, :, lanes]
                    total = total + (value if term is None else term[:, lanes] * value)
                target[g, :, lanes] = total

    def own_matrix(g, f, at):
        return coef_ref[g, f : f + 1, at]

    def scaled_cube(g, f, at):
        return cube_ref[1, g, f : f + 1, at]

    def cube(g, f, at):
        return cube_ref[0, g, f : f + 1, at]

    moments = [mom_ref[j] for j in range(POWERS)]
    lifted = []
    copies = []
    poly = []
    heights = []
    for level in range(levels):
        count = len(moments)
        p1 = [times(moments[j + 1]) for j in range(count - 1)]
        sent = jnp.concatenate(
            [moments[0], p1[0], times(p1[1] - tau[1] * moments[0])], axis=0
        )
        sums = seg_sum(sent, hot_ref[level])
        for block in range(2):
            part_ref[level, block] = sums[:, (1 + block) * pair : (2 + block) * pair]
        going = [
            remote(part_ref.at[level, k // 2], part_in.at[level, k], levels + level, k)
            for k in range(4)
        ]
        for copy in going:
            copy.start()

        p2 = [times(p1[j + 1]) for j in range(count - 2)]
        p3 = [times(p2[j + 1]) for j in range(count - 3)]
        if level == 0:
            for later in range(1, levels):
                build_hot(later)
                stat_copies.append(send_stat(later))
            operator(0, a)
            operator(1, a3)
        elif level == 1:
            apply(0, own_matrix, v1_ref, v2_ref, [], [])
        else:
            z = [poly[6], poly[7], poly[8]]
            apply(1, scaled_cube, state_ref, out_ref, z, [state_ref, v1_ref, v2_ref])
            z = [poly[3], poly[4], poly[5]]
            apply(1, cube, out_ref, out_ref, z, [state_ref, v1_ref, v2_ref])

        for copy in stat_copies[level]:
            copy.wait_recv()
        for copy in going:
            copy.wait_recv()
        own = sums[:, :pair] + part_in[level, 0] + part_in[level, 2]
        own = own + pltpu.roll(part_in[level, 1] + part_in[level, 3], tent_dev, 1)
        stat = stat_ref[level, 0] + stat_in[level, 0] + stat_in[level, 2]
        stat = stat + pltpu.roll(stat_in[level, 1] + stat_in[level, 3], tent_dev, 1)
        per = 1.0 / jnp.maximum(stat[fields * fields : fields * fields + 1], 1.0)
        tot_ref[level, 0 : 2 * GROUP, :] = own[: 2 * GROUP] * per
        tot_ref[level, 2 * GROUP :, :] = jnp.zeros((GROUP, pair), F32)
        for g in range(fields):
            joint = stat[g * fields : g * fields + 1] * (own[0:1] * per)
            for f in range(1, fields):
                joint = joint + stat[g * fields + f : g * fields + f + 1] * (
                    own[f : f + 1] * per
                )
            row = 2 * GROUP + g
            tot_ref[level, row : row + 1, :] = (
                own[row : row + 1] + tau[1] * joint
            ) * per
        back = [
            remote(tot_ref.at[level], tot_in.at[level, k], 2 * levels + level, k)
            for k in range(4)
        ]
        for copy in back:
            copy.start()
        copies += going + back

        if level == 0:
            arrived = [stat_in[0, k, crows:, :] for k in range(4)]
            table = table_of(stat_ref[0, 0, crows:, :], arrived)
            for later in range(levels):
                found = seg_take(table, hot_ref[later])
                heights.append(found[later : later + 1])
            poly = [None]
            for h in heights:
                by = [h, h * h * 0.5, h * h * h * (1.0 / 6.0)]
                longer = list(poly) + [0.0] * 3
                for i, value in enumerate(poly):
                    for k in range(3):
                        term = by[k] if value is None else value * by[k]
                        longer[i + k + 1] = longer[i + k + 1] + term
                poly = longer
            apply(0, own_matrix, state_ref, v1_ref, [], [])
        elif level == 1:
            for g in range(fields):
                row = coef_ref[g]
                for _ in range(2):
                    total = row[0:1] * coef_ref[0]
                    for f in range(1, fields):
                        total = total + row[f : f + 1] * coef_ref[f]
                    row = total
                cube_ref[0, g] = row
                cube_ref[1, g] = row * poly[9]
        else:
            z = [None, poly[1], poly[2]]
            apply(1, cube, out_ref, out_ref, z, [state_ref, v1_ref, v2_ref])
        h = heights[level]
        h2 = h * h * 0.5
        h3 = h * h * h * (1.0 / 6.0)
        still = [
            moments[j] + h * p1[j] + h2 * p2[j] + h3 * p3[j] for j in range(count - 3)
        ]
        grown = list(lifted) + [0.0] * 3
        power = list(lifted)
        for k, weight in enumerate([h, h2, h3]):
            power = [times(v) for v in power]
            for j, v in enumerate(power):
                grown[j + k + 1] = grown[j + k + 1] + weight * v
        if level == levels - 1:
            l0 = lift_row
            l1 = dot3(l0, a, NT)
            l2 = dot3(l0, a2, NT)
            l02 = jnp.concatenate([l0, l1, l2], axis=0)
            l35 = dot3(l02, a3, NT)
            l68 = dot3(l35, a3, NT)
            ladder = jnp.concatenate(
                [l02, l35, l68, jnp.zeros((16 - POWERS, basis), F32)], axis=0
            )
            ladder = jnp.concatenate(
                [ladder, jnp.zeros((16, wide - basis), F32)], axis=1
            )
            l_hi, l_lo = split2(ladder)
            l_hi = l_hi.astype(F32)
            ladder = jnp.concatenate(
                [l_hi, l_hi, l_lo.astype(F32), jnp.zeros((wide - 48, wide), F32)],
                axis=0,
            ).T.astype(BF16)
            fin_ref[...] = jnp.zeros_like(fin_ref)

        for copy in back:
            copy.wait_recv()
        each = seg_take(
            table_of(tot_ref[level], [tot_in[level, k] for k in range(4)]),
            hot_ref[level],
        )
        d0 = each[:GROUP] - moments[0]
        d1 = each[GROUP : 2 * GROUP] - (p1[0] + tau[0] * d0)
        cd0 = times(d0)
        d2 = each[2 * GROUP :] - (p2[0] + tau[1] * cd0 + tau[0] * d1)
        q = [
            h * d0 + h2 * d1 + h3 * d2,
            h2 * cd0 + h3 * times(d1),
            h3 * times(cd0),
        ]
        moments = [
            still[j] + tau[j] * q[0] + tau[j + 1] * q[1] + tau[j + 2] * q[2]
            for j in range(count - 3)
        ]
        for j in range(3):
            grown[j] = grown[j] + q[j]
        lifted = grown

    for j in range(POWERS):
        for f in range(fields):
            fin_ref[f, j : j + 1, :] = lifted[j][f : f + 1]
    for f in range(fields):
        c_hi, c_lo = split2(fin_ref[f])
        rhs = jnp.concatenate([c_hi, c_lo, c_hi], axis=0)
        res = jnp.dot(ladder[:, :48], rhs, preferred_element_type=F32)
        out_ref[f] = out_ref[f] + res[:basis]
    for group in stat_copies:
        for copy in group:
            copy.wait_send()
    for copy in copies:
        copy.wait_send()


def per_device(
    sizes, state, coef, basis_quad, test_deriv, trace_vec, lift_vec, tent_height, elem_tent
):
    fields, basis, n_elem = state.shape
    levels, tent_dev = tent_height.shape
    pair = 2 * tent_dev
    wide = up(basis, LANES)
    crows = up(fields * fields + 1, 8)
    srows = crows + up(levels, 8)
    vmem = pl.BlockSpec(memory_space=pltpu.VMEM)
    hbm = pl.BlockSpec(memory_space=pltpu.HBM)
    operands = (
        state,
        coef,
        basis_quad,
        test_deriv.T,
        trace_vec.reshape(1, basis),
        lift_vec.reshape(1, basis),
        tent_height,
        elem_tent,
    )
    return pl.pallas_call(
        functools.partial(kernel, sizes),
        out_shape=jax.ShapeDtypeStruct(state.shape, F32),
        in_specs=[hbm] * 8,
        out_specs=vmem,
        scratch_shapes=[pltpu.VMEM(x.shape, x.dtype) for x in operands]
        + [
            pltpu.VMEM((levels, 3 * pair, n_elem), BF16),
            pltpu.VMEM((2, 2 * wide, 2 * wide), BF16),
            pltpu.VMEM((crows, n_elem), F32),
            pltpu.VMEM((fields, GROUP, n_elem), F32),
            pltpu.VMEM((2, fields, fields, n_elem), F32),
            pltpu.VMEM((POWERS, GROUP, n_elem), F32),
            pltpu.VMEM((fields, 16, n_elem), F32),
            pltpu.VMEM(state.shape, F32),
            pltpu.VMEM(state.shape, F32),
            pltpu.VMEM((fields, 2 * wide, n_elem), BF16),
            pltpu.VMEM((levels, 3, srows, pair), F32),
            pltpu.VMEM((levels, 4, srows, pair), F32),
            pltpu.VMEM((levels, 2, 3 * GROUP, pair), F32),
            pltpu.VMEM((levels, 4, 3 * GROUP, pair), F32),
            pltpu.VMEM((levels, 3 * GROUP, pair), F32),
            pltpu.VMEM((levels, 4, 3 * GROUP, pair), F32),
            pltpu.SemaphoreType.DMA((8,)),
            pltpu.SemaphoreType.DMA((3 * levels, 4)),
            pltpu.SemaphoreType.DMA((3 * levels, 4)),
        ],
        compiler_params=pltpu.CompilerParams(
            collective_id=0, has_side_effects=True, vmem_limit_bytes=63 * 1024 * 1024
        ),
    )(*operands)


def solution(mesh):
    split = ("gx", "gy")
    placed = (
        P(None, None, split),
        P(None, None, split),
        P(),
        P(),
        P(),
        P(),
        P(None, split),
        P(None, split),
    )
    sizes = (mesh.shape["gx"], mesh.shape["gy"])
    return jax.shard_map(
        functools.partial(per_device, sizes),
        mesh=mesh,
        in_specs=placed,
        out_specs=P(None, None, split),
        check_vma=False,
    )
```

time: 45.9 us -> 38.2 us (0.83)
  local copies, waits for them, and re-layouts: 7.77 us -> 2.4 us
  Pallas kernels: 37.8 us -> 35.6 us
    unnamed x16 -> x1, local copies, waits for them, and re-layouts: 7.77 us -> 2.4 us
    pallas_call x1, Pallas kernels: 37.8 us -> 35.6 us  [per_device(): pl.pallas_call(functools.partial(kernel, sizes), out_shape=jax.ShapeDtype...]
where the time goes in v2:
time: 38.2 us; the launch traced here: 38 us
  Pallas kernels  35.6 us (93%)
  local copies, waits for them, and re-layouts  2.4 us (6%)
    pallas_call x1, Pallas kernels, per_device(): pl.pallas_call(functools.partial(kernel, sizes), out_shape=jax.ShapeDtype...  35.6 us
    unnamed x1, local copies, waits for them, and re-layouts  2.4 us

profile of v2, /device:TPU:0, one launch (start us, length us, event | category | flops | bytes accessed | tf_op | source)
XLA Modules:
  0.0 38.0 jit_solution(15143012820003113820)
XLA Ops:
  0.0 35.6 %shard_map.82 = f32[5,120,512]{2,1,0:T(8,128)} custom-call(f32[5,120,512]{2,1,0:T(8,128)} %state_hbm.1, f32[5,5,512]{2,1,0:T(8,128)} %coef_hbm.1, f32[216,120]{1,0:T(8,128)} %bq_hbm.1, f32[216,120]{1,0:T(8,128)} %bitcast.3, f32[1,120]{1,0:T(1,128)} %bitcast.4, f32[1,120]{1,0:T(1,128)} %bitcast.5, f32[3,64]{1,0:T(4,128)} %height_hbm.1, s32[3,512]{1,0:T(4,128)} %tent_hbm.1), custom_call_target="tpu_custom_call" | custom-call | tf_op jit(solution)/shard_map/pallas_call | solution.py:497
  35.6 2.4 %copy.10 = f32[5,120,512]{2,1,0:T(8,128)} copy(f32[5,120,512]{2,1,0:T(8,128)} %shard_map.82) | data formatting | bytes 2457600

commit v3 on v2

--- a/solution.py
+++ b/solution.py
@@ -76,6 +76,9 @@
     lift_hbm,
     height_hbm,
     tent_hbm,
+    still_hbm,
+    fin_ref,
+    ladder_ref,
     out_ref,
     state_ref,
     coef_ref,
@@ -91,7 +94,6 @@
     ct_ref,
     cube_ref,
     mom_ref,
-    fin_ref,
     v1_ref,
     v2_ref,
     g_ref,
@@ -102,6 +104,7 @@
     tot_ref,
     tot_in,
     load_sem,
+    save_sem,
     send_sem,
     recv_sem,
 ):
@@ -339,8 +342,6 @@
         elif level == 1:
             apply(0, own_matrix, v1_ref, v2_ref, [], [])
         else:
-            z = [poly[6], poly[7], poly[8]]
-            apply(1, scaled_cube, state_ref, out_ref, z, [state_ref, v1_ref, v2_ref])
             z = [poly[3], poly[4], poly[5]]
             apply(1, cube, out_ref, out_ref, z, [state_ref, v1_ref, v2_ref])
 
@@ -399,9 +400,13 @@
                     row = total
                 cube_ref[0, g] = row
                 cube_ref[1, g] = row * poly[9]
+            z = [poly[6], poly[7], poly[8]]
+            apply(1, scaled_cube, state_ref, out_ref, z, [state_ref, v1_ref, v2_ref])
         else:
             z = [None, poly[1], poly[2]]
             apply(1, cube, out_ref, out_ref, z, [state_ref, v1_ref, v2_ref])
+            save = pltpu.make_async_copy(out_ref, still_hbm, save_sem.at[0])
+            save.start()
         h = heights[level]
         h2 = h * h * 0.5
         h3 = h * h * h * (1.0 / 6.0)
@@ -429,7 +434,7 @@
             )
             l_hi, l_lo = split2(ladder)
             l_hi = l_hi.astype(F32)
-            ladder = jnp.concatenate(
+            ladder_ref[...] = jnp.concatenate(
                 [l_hi, l_hi, l_lo.astype(F32), jnp.zeros((wide - 48, wide), F32)],
                 axis=0,
             ).T.astype(BF16)
@@ -461,16 +466,19 @@
     for j in range(POWERS):
         for f in range(fields):
             fin_ref[f, j : j + 1, :] = lifted[j][f : f + 1]
-    for f in range(fields):
-        c_hi, c_lo = split2(fin_ref[f])
-        rhs = jnp.concatenate([c_hi, c_lo, c_hi], axis=0)
-        res = jnp.dot(ladder[:, :48], rhs, preferred_element_type=F32)
-        out_ref[f] = out_ref[f] + res[:basis]
+    save.wait()
     for group in stat_copies:
         for copy in group:
             copy.wait_send()
     for copy in copies:
         copy.wait_send()
+
+
+def add_fluxes(still_ref, fin_ref, ladder_ref, out_ref):
+    c_hi, c_lo = split2(fin_ref[0])
+    rhs = jnp.concatenate([c_hi, c_lo, c_hi], axis=0)
+    res = jnp.dot(ladder_ref[:, :48], rhs, preferred_element_type=F32)
+    out_ref[0] = still_ref[0] + res[: out_ref.shape[1]]
 
 
 def per_device(
@@ -494,12 +502,17 @@
         tent_height,
         elem_tent,
     )
-    return pl.pallas_call(
+    still, fluxes, ladder = pl.pallas_call(
         functools.partial(kernel, sizes),
-        out_shape=jax.ShapeDtypeStruct(state.shape, F32),
+        out_shape=[
+            jax.ShapeDtypeStruct(state.shape, F32),
+            jax.ShapeDtypeStruct((fields, 16, n_elem), F32),
+            jax.ShapeDtypeStruct((wide, wide), BF16),
+        ],
         in_specs=[hbm] * 8,
-        out_specs=vmem,
-        scratch_shapes=[pltpu.VMEM(x.shape, x.dtype) for x in operands]
+        out_specs=[hbm, vmem, vmem],
+        scratch_shapes=[pltpu.VMEM(state.shape, F32)]
+        + [pltpu.VMEM(x.shape, x.dtype) for x in operands]
         + [
             pltpu.VMEM((levels, 3 * pair, n_elem), BF16),
             pltpu.VMEM((2, 2 * wide, 2 * wide), BF16),
@@ -507,7 +520,6 @@
             pltpu.VMEM((fields, GROUP, n_elem), F32),
             pltpu.VMEM((2, fields, fields, n_elem), F32),
             pltpu.VMEM((POWERS, GROUP, n_elem), F32),
-            pltpu.VMEM((fields, 16, n_elem), F32),
             pltpu.VMEM(state.shape, F32),
             pltpu.VMEM(state.shape, F32),
             pltpu.VMEM((fields, 2 * wide, n_elem), BF16),
@@ -518,6 +530,7 @@
             pltpu.VMEM((levels, 3 * GROUP, pair), F32),
             pltpu.VMEM((levels, 4, 3 * GROUP, pair), F32),
             pltpu.SemaphoreType.DMA((8,)),
+            pltpu.SemaphoreType.DMA((1,)),
             pltpu.SemaphoreType.DMA((3 * levels, 4)),
             pltpu.SemaphoreType.DMA((3 * levels, 4)),
         ],
@@ -525,6 +538,18 @@
             collective_id=0, has_side_effects=True, vmem_limit_bytes=63 * 1024 * 1024
         ),
     )(*operands)
+    return pl.pallas_call(
+        add_fluxes,
+        grid=(fields,),
+        out_shape=jax.ShapeDtypeStruct(state.shape, F32),
+        in_specs=[
+            pl.BlockSpec((1, basis, n_elem), lambda f: (f, 0, 0)),
+            pl.BlockSpec((1, 16, n_elem), lambda f: (f, 0, 0)),
+            pl.BlockSpec((wide, wide), lambda f: (0, 0)),
+        ],
+        out_specs=pl.BlockSpec((1, basis, n_elem), lambda f: (f, 0, 0)),
+        compiler_params=pltpu.CompilerParams(vmem_limit_bytes=63 * 1024 * 1024),
+    )(still, fluxes, ladder)
 
 
 def solution(mesh):

time: 38.2 us -> 39.5 us (1.034)
  Pallas kernels: 35.6 us -> 39.3 us
  local copies, waits for them, and re-layouts: 2.4 us -> 0 us
    pallas_call x1 -> x2, Pallas kernels: 35.6 us -> 39.3 us  [the longest x1 35 us: per_device(): pl.pallas_call(functools.partial(kernel, sizes), out_shape=[jax.ShapeDtyp...]
    unnamed x1 -> x0, local copies, waits for them, and re-layouts: 2.4 us -> none
where the time goes in v3:
time: 39.5 us; the launch traced here: 39.3 us
  Pallas kernels  39.3 us (99%)
    pallas_call x1, Pallas kernels, per_device(): pl.pallas_call(functools.partial(kernel, sizes), out_shape=[jax.ShapeDtyp...  35 us
    pallas_call x1, Pallas kernels, per_device(): pl.pallas_call(add_fluxes, grid=(fields,), out_shape=jax.ShapeDtypeStruct...  4.33 us

profile of v3, /device:TPU:0, one launch (start us, length us, event | category | flops | bytes accessed | tf_op | source)
XLA Modules:
  0.0 39.3 jit_solution(5563125282986911910)
XLA Ops:
  0.0 35.0 %shard_map.82 = (f32[5,120,512]{2,1,0:T(8,128)}, f32[5,16,512]{2,1,0:T(8,128)}, bf16[128,128]{1,0:T(8,128)(2,1)}) custom-call(f32[5,120,512]{2,1,0:T(8,128)} %state_hbm.1, f32[5,5,512]{2,1,0:T(8,128)} %coef_hbm.1, f32[216,120]{1,0:T(8,128)} %bq_hbm.1, f32[216,120]{1,0:T(8,128)} %bitcast.3, f32[1,120]{1,0:T(1,128)} %bitcast.4, f32[1,120]{1,0:T(1,128)} %bitcast.5, ...), custom_call_target="tpu_custom_call" | custom-call | tf_op jit(solution)/shard_map/pallas_call | solution.py:505
  35.0 4.3 %shard_map.83 = f32[5,120,512]{2,1,0:T(8,128)} custom-call(f32[5,120,512]{2,1,0:T(8,128)} %get-tuple-element.8.still_ref, f32[5,16,512]{2,1,0:T(8,128)} %get-tuple-element.9.fin_ref, bf16[128,128]{1,0:T(8,128)(2,1)} %get-tuple-element.10.ladder_ref), custom_call_target="tpu_custom_call" | custom-call | tf_op jit(solution)/shard_map/pallas_call | solution.py:541
